TPU v7x, 256 devices: a whole 4x4x8 slice. The times are simulated.
256 devices in a mesh: dp: 16 (over y, z_hi), tp: 16 (over x, z_lo, core).
Axes of the slice: x: 4, y: 4, z: 8 (z_hi: 4, z_lo: 2; z = z_hi * 2 + z_lo), core: 2. Of those that a mesh axis runs over, the one named last changes fastest.
Arguments:
- inputs: bfloat16 [12288, 8192], P('dp', 'tp'), may hold values from -6 to 6
- gate_pre: bfloat16 [12288, 14336], P('dp', 'tp'), may hold values from -6 to 6
- up_pre: bfloat16 [12288, 14336], P('dp', 'tp'), may hold values from -6 to 6
- out_grads: bfloat16 [12288, 8192], P('dp', 'tp'), may hold values from -6 to 6
- down_weight: bfloat16 [14336, 8192], P('tp', 'dp'), may hold values from -0.0625 to 0.0625
- example_ids: int32 [12288], P('dp'), may hold values from 0 to 63, as said below
- input_factor: bfloat16 [8192, 64], P('tp'), may hold values from -0.5 to 0.5
- gate_factor: bfloat16 [14336, 64], P('tp'), may hold values from -0.5 to 0.5
- up_factor: bfloat16 [14336, 64], P('tp'), may hold values from -0.5 to 0.5
- hidden_factor: bfloat16 [14336, 64], P('tp'), may hold values from -0.5 to 0.5
- output_factor: bfloat16 [8192, 64], replicated, may hold values from -0.5 to 0.5
- queries: bfloat16 [8192, 4096], P(('dp', 'tp')), may hold values from -6 to 6
Outputs:
- scores: float32 [64, 8192], P(None, ('dp', 'tp'))
Inputs may be any that keep to these rules, and one draw needn't show every extreme that they name: `example_ids`: the tokens of index b of dp carry the example ids b * 4 to b * 4 + 3, never falling along the tokens, each id on at least one token.
All inputs are finite; a program needn't handle non-finite values.
Results may differ from a plain program's by a relative error of at most 0.0029.
Values may be sent and summed in bfloat16 or wider, within the bound.
A program may use at most 128 MiB of HBM per device.

v0:
```python
import jax
import jax.numpy as jnp
from jax import lax
from jax.sharding import PartitionSpec as P

R = 64
EX_DEV = 4


def outer_sums(member_mask, left_proj, right_proj):
    return jnp.einsum(
        "et,ti,tj->eij", member_mask, left_proj, right_proj, precision=lax.Precision.HIGHEST
    )


def local(
    inputs,
    gate_pre,
    up_pre,
    out_grads,
    down_weight,
    example_ids,
    input_factor,
    gate_factor,
    up_factor,
    hidden_factor,
    output_factor,
    queries,
):
    full_grads = lax.all_gather(out_grads, "tp", axis=1, tiled=True)
    hidden_grad = lax.dot_general(
        full_grads,
        lax.all_gather(down_weight, "dp", axis=1, tiled=True),
        (((1,), (1,)), ((), ())),
        preferred_element_type=jnp.float32,
    )
    gate_values = gate_pre.astype(jnp.float32)
    up_values = up_pre.astype(jnp.float32)
    gate_sigmoid = jax.nn.sigmoid(gate_values)
    activated = gate_values * gate_sigmoid
    hidden = activated * up_values
    gate_grad = hidden_grad * up_values * gate_sigmoid * (1.0 + gate_values * (1.0 - gate_sigmoid))
    up_grad = hidden_grad * activated
    input_local = jnp.dot(inputs, input_factor, preferred_element_type=jnp.float32)
    output_proj = jnp.dot(full_grads, output_factor, preferred_element_type=jnp.float32)
    grad_local = jnp.dot(
        gate_grad, gate_factor.astype(jnp.float32), precision=lax.Precision.HIGHEST
    ) + jnp.dot(up_grad, up_factor.astype(jnp.float32), precision=lax.Precision.HIGHEST)
    hidden_local = jnp.dot(
        hidden, hidden_factor.astype(jnp.float32), precision=lax.Precision.HIGHEST
    )
    wanted = lax.axis_index("dp") * EX_DEV + jnp.arange(EX_DEV, dtype=jnp.int32)
    member_mask = (example_ids[None, :] == wanted[:, None]).astype(jnp.float32)
    input_proj, grad_proj, hidden_proj = lax.psum((input_local, grad_local, hidden_local), "tp")
    sketch = outer_sums(member_mask, input_proj, grad_proj) + outer_sums(
        member_mask, hidden_proj, output_proj
    )
    sketch = sketch.reshape(EX_DEV, R * R)
    mean_square = jnp.mean(sketch * sketch, axis=1, keepdims=True)
    unit_sketch = (sketch * lax.rsqrt(mean_square + 1e-06)).astype(jnp.bfloat16)
    score_scale = 1.0 / R
    every_unit = lax.all_gather(unit_sketch, "dp", axis=0, tiled=True)
    products = lax.dot_general(
        every_unit, queries, (((1,), (1,)), ((), ())), preferred_element_type=jnp.float32
    )
    return products * score_scale


def solution(mesh):
    return jax.shard_map(
        local,
        mesh=mesh,
        in_specs=(
            P("dp", "tp"),
            P("dp", "tp"),
            P("dp", "tp"),
            P("dp", "tp"),
            P("tp", "dp"),
            P("dp"),
            P("tp", None),
            P("tp", None),
            P("tp", None),
            P("tp", None),
            P(),
            P(("dp", "tp"), None),
        ),
        out_specs=P(None, ("dp", "tp")),
        check_vma=False,
    )
```

profile of v0, /device:TPU:1, one launch (start us, length us, event | category | flops | bytes accessed | tf_op | source)
XLA Modules:
  0.0 474.0 jit_solution(11462394547164257233)
XLA Ops:
  6.5 0.0 copy-start
  6.5 0.0 all-gather.4.cloned.1.call-start
  6.5 0.7 all-gather.4.cloned.1.call-update
  7.3 0.0 all-gather.6.cloned.1.call-start
  7.3 0.7 all-gather.6.cloned.1.call-update
  8.0 0.0 all-reduce.3.cloned.1.call-start
  8.1 0.8 convert_bitcast_fusion
  8.8 2.2 fusion.31
  11.0 0.0 copy-done.2
  11.0 0.0 copy-done.4
  11.0 4.3 fusion.4
  15.3 72.6 %all-gather.4.cloned.1.call-done = bf16[768,8192]{1,0:T(8,128)(2,1)} async-done(((bf16[768,512]{1,0:T(8,128)(2,1)}), bf16[768,8192]{1,0:T(8,128)(2,1)}) %all-gather.4.cloned.1.call-update) | async-done | bytes 12582928 | tf_op jit(solution)/shard_map/all_gather | solution.py:30
  87.9 191.0 %all-gather.6.cloned.1.call-done = bf16[896,8192]{1,0:T(8,128)(2,1)} async-done(((bf16[896,512]{1,0:T(8,128)(2,1)}), bf16[896,8192]{1,0:T(8,128)(2,1)}) %all-gather.6.cloned.1.call-update) | async-done | bytes 14680080 | tf_op jit(solution)/shard_map/all_gather | solution.py:33
  278.9 17.8 %fusion.32 = f32[768,896]{1,0:T(8,128)S(1)} fusion(bf16[768,8192]{1,0:T(8,128)(2,1)} %all-gather.4.cloned.1.call-done, bf16[896,8192]{1,0:T(8,128)(2,1)} %all-gather.6.cloned.1.call-done), kind=kOutput, calls=%fused_computation.40 | convolution fusion | flops 11274289152 | bytes 30015488 | tf_op jit(solution)/shard_map/dot_general | solution.py:31
  296.6 0.0 copy-done.5
  296.6 0.0 copy-start.3
  296.6 0.0 copy-start.6
  296.7 2.2 fusion.10
  298.9 0.0 copy-done.3
  298.9 0.0 copy-done.6
  298.9 3.3 fusion.15
  302.2 0.0 all-reduce.3.cloned.1.call-update
  302.2 0.0 copy-done
  302.3 8.5 %convolution_bitcast_fusion = f32[768,64,1]{0,1,2:T(8,128)S(1)} fusion(bf16[768,8192]{1,0:T(8,128)(2,1)} %all-gather.4.cloned.1.call-done, bf16[8192,64]{0,1:T(8,128)(2,1)S(1)} %copy-done), kind=kOutput, calls=%fused_computation.17 | convolution fusion | flops 805306368 | bytes 13828096 | tf_op jit(solution)/shard_map/dot_general | solution.py:45
  310.8 111.6 %all-reduce.3.cloned.1.call-done = (f32[768,64]{0,1:T(8,128)}, f32[768,64]{0,1:T(8,128)}, f32[768,64]{0,1:T(8,128)}) async-done(((f32[768,64]{0,1:T(8,128)}, f32[768,64]{0,1:T(8,128)}, f32[768,64]{0,1:T(8,128)}), (f32[768,64]{0,1:T(8,128)}, f32[768,64]{0,1:T(8,128)}, f32[768,64]{0,1:T(8,128)})) %all-reduce.3.cloned.1.call-update) | async-done | bytes 589840 | tf_op jit(solution)/shard_map/psum | solution.py:54
  422.4 1.8 fusion.20
  424.2 1.8 multiply_reduce_fusion
  426.0 0.1 reshape.16
  426.1 0.1 fusion.27
  426.2 40.3 %all-gather = bf16[16,4,4096]{2,1,0:T(4,128)(2,1)S(1)} all-gather(bf16[1,4,4096]{2,1,0:T(4,128)(2,1)S(1)} %fusion.27), channel_id=1, replica_groups=mesh['dp'=16,'tp'=16] {'dp'}, dimensions={0}, use_global_device_ids=true | all-gather | bytes 557056 | tf_op jit(solution)/shard_map/all_gather | solution.py:62
  466.5 0.1 reshape.18
  466.6 0.9 convolution_multiply_fusion
  (7 shorter events, 0.0 us)
Async XLA Ops:
  6.5 295.7 %copy-start = (bf16[8192,64]{0,1:T(8,128)(2,1)S(1)}, bf16[8192,64]{0,1:T(8,128)(2,1)}, u32[]{:S(2)}) copy-start(bf16[8192,64]{0,1:T(8,128)(2,1)} %param.22) | copy-start | bytes 3145732
  6.5 4.5 copy-start.2
  6.5 4.5 copy-start.4
  6.5 81.4 %all-gather.4.cloned.1.call-start = ((), (), s32[]{:S(2)}) async-start(), calls=%async_computation | async-start | bytes 13369344 | tf_op jit(solution)/shard_map/all_gather | solution.py:30
  7.3 271.6 %all-gather.6.cloned.1.call-start = ((), (), s32[]{:S(2)}) async-start(), calls=%async_computation.1 | async-start | bytes 15597568 | tf_op jit(solution)/shard_map/all_gather | solution.py:33
  8.0 414.4 %all-reduce.3.cloned.1.call-start = ((), (), s32[]{:S(2)}) async-start(), calls=%async_computation.2 | async-start | bytes 1179648 | tf_op jit(solution)/shard_map/psum | solution.py:54
  15.3 281.3 %copy-start.5 = (bf16[896,64]{0,1:T(8,128)(2,1)S(1)}, bf16[896,64]{0,1:T(8,128)(2,1)}, u32[]{:S(2)}) copy-start(bf16[896,64]{0,1:T(8,128)(2,1)} %param.20) | copy-start | bytes 344068
  296.6 2.3 copy-start.3
  296.6 2.3 copy-start.6
  310.8 155.8 %copy-start.1 = (bf16[32,4096]{1,0:T(8,128)(2,1)S(1)}, bf16[32,4096]{1,0:T(8,128)(2,1)}, u32[]{:S(2)}) copy-start(bf16[32,4096]{1,0:T(8,128)(2,1)} %param.23) | copy-start | bytes 786436
Sparse Core Ops, SparseCore 0:
  9.2 78.6 all-gather.3
  90.3 188.5 all-gather.5
  302.4 119.9 all-reduce.2
where the time goes:
time: 481 us; the launch traced here: 474 us
  waiting for transfers between devices  377 us (78%)
  matrix products  42.7 us (9%)
  blocking collectives  40.3 us (8%)
  between operations  13.2 us (3%)
    all_gather x1, waiting for transfers between devices, local(): lax.all_gather(down_weight, 'dp', axis=1, tiled=True)  191 us
    psum x1, waiting for transfers between devices, local(): lax.psum((input_local, grad_local, hidden_local), 'tp')  112 us
    all_gather x1, waiting for transfers between devices, local(): full_grads = lax.all_gather(out_grads, 'tp', axis=1, tiled=True)  72.6 us
    all_gather x1, blocking collectives, local(): every_unit = lax.all_gather(unit_sketch, 'dp', axis=0, tiled=True)  40.3 us
    dot_general x1, matrix products, local(): lax.dot_general(full_grads, lax.all_gather(down_weight, 'dp', axis=1, til...  17.8 us
  transfers between devices with their start and end apart: 3, of which 3 were waited for; matrix products, arithmetic and copies ran while one was open for 3% of the time, Pallas kernels for 0%

commit v1 on v0

v1 whole, which is shorter than its diff:
```python
import functools

import jax
import jax.numpy as jnp
from jax import lax
from jax.experimental import pallas as pl
from jax.experimental.pallas import tpu as pltpu
from jax.sharding import PartitionSpec as P

TOK = 768
DS = 512
FS = 896
CH = 128
NCH = FS // CH
HALF = CH // 2
N = 16
MESH = pl.DeviceIdType.MESH
HIGHEST = lax.Precision.HIGHEST
NT = (((1,), (1,)), ((), ()))


def dot(a, b, precision=None):
    return jnp.dot(a, b, preferred_element_type=jnp.float32, precision=precision)


def dot_nt(a, b, precision=None):
    return lax.dot_general(a, b, NT, preferred_element_type=jnp.float32, precision=precision)


def split(x):
    hi = x.astype(jnp.bfloat16)
    lo = (x - hi.astype(jnp.float32)).astype(jnp.bfloat16)
    return hi, lo


def iota2(shape):
    return (
        lax.broadcasted_iota(jnp.int32, shape, 0),
        lax.broadcasted_iota(jnp.int32, shape, 1),
    )


def spread(kind):
    row, col = iota2((64, 128))
    hit = (row == ((col >> 3) << 2) + (col & 3)) & (((col >> 2) & 1) == kind)
    return jnp.where(hit, 1.0, 0.0).astype(jnp.bfloat16)


def kernel(
    in_hbm, gate_hbm, up_hbm, og_hbm, w_hbm, ids_ref, inf_ref, gf_ref, uf_ref, hf_ref, of_hbm, q_hbm,
    out_ref,
    ogb, wb, inb, gb, ub, ofb, qb, ab, fp, acc, pih_msg, pih_rcv, iph, opt, gmat, omat, t2,
    gacc, gmsg, grcv, pall, qj, scm, scr,
    loc_sem, zs_s, zs_r, ys_s, ys_r, oz_s, oz_r, ox_s, ox_r, oc_s, oc_r, small_s, small_r,
):
    dp, tp = lax.axis_index("dp"), lax.axis_index("tp")
    x, zl, core = tp >> 2, (tp >> 1) & 1, tp & 1
    y, zh = dp >> 2, dp & 3

    def dev(d, t):
        return {"dp": d, "tp": t}

    def remote(src, dst, ss, rs, d, t):
        return pltpu.make_async_remote_copy(
            src_ref=src, dst_ref=dst, send_sem=ss, recv_sem=rs,
            device_id=dev(d, t), device_id_type=MESH,
        )

    pending = []

    def send(src, dst, ss, rs, d, t):
        copy = remote(src, dst, ss, rs, d, t)
        copy.start()
        pending.append(copy)

    def arrived(dst, rs):
        remote(dst, dst, rs, rs, dp, tp ^ 1).wait_recv()

    loads = []
    for n, (src, dst) in enumerate((
        (w_hbm, wb.at[dp]), (og_hbm, ogb.at[tp]), (in_hbm, inb), (gate_hbm, gb), (up_hbm, ub),
        (q_hbm, qb), (of_hbm, ofb),
    )):
        copy = pltpu.make_async_copy(src, dst, loc_sem.at[n])
        copy.start()
        loads.append(copy)
    barrier = pltpu.get_barrier_semaphore()
    for k in range(1, N):
        pl.semaphore_signal(barrier, 1, device_id=dev(dp, tp ^ k), device_id_type=MESH)
        pl.semaphore_signal(barrier, 1, device_id=dev(dp ^ k, tp), device_id_type=MESH)
    pl.semaphore_wait(barrier, 2 * (N - 1))
    loads[0].wait()
    loads[1].wait()

    zh_up, zh_down = (zh + 1) & 3, (zh + 3) & 3
    y_up, y_down = (y + 1) & 3, (y + 3) & 3
    zh_of = (zh, zh_down, zh_up, (zh + 2) & 3)

    def at(yy, zz):
        return yy * 4 + zz

    def rows(i, part=None):
        if part is None:
            return pl.ds(i * CH, CH)
        return pl.ds(i * CH + part * HALF, HALF)

    def w_send(block, r, sems, idx, target):
        ss, rs = sems
        ref = wb.at[block, r]
        send(ref, ref, ss.at[idx], rs.at[idx], target, tp)

    def z_own(i):
        w_send(dp, rows(i), (zs_s, zs_r), 4 * i, at(y, zh_up))
        w_send(dp, rows(i), (zs_s, zs_r), 4 * i + 1, at(y, zh_down))

    def z_forward(i):
        arrived(wb.at[at(y, zh_down), rows(i)], zs_r.at[4 * i])
        w_send(at(y, zh_down), rows(i, 0), (zs_s, zs_r), 4 * i + 2, at(y, zh_up))
        arrived(wb.at[at(y, zh_up), rows(i)], zs_r.at[4 * i + 1])
        w_send(at(y, zh_up), rows(i, 1), (zs_s, zs_r), 4 * i + 3, at(y, zh_down))

    def z_last(i):
        for part in range(2):
            arrived(wb.at[at(y, zh_of[3]), rows(i, part)], zs_r.at[4 * i + 2 + part])

    def y_send(i, q):
        base = 16 * i + 4 * q
        w_send(at(y, zh_of[q]), rows(i), (ys_s, ys_r), base, at(y_up, zh))
        w_send(at(y, zh_of[q]), rows(i), (ys_s, ys_r), base + 1, at(y_down, zh))

    def y_forward(i, q):
        base = 16 * i + 4 * q
        arrived(wb.at[at(y_down, zh_of[q]), rows(i)], ys_r.at[base])
        w_send(at(y_down, zh_of[q]), rows(i, 0), (ys_s, ys_r), base + 2, at(y_up, zh))
        arrived(wb.at[at(y_up, zh_of[q]), rows(i)], ys_r.at[base + 1])
        w_send(at(y_up, zh_of[q]), rows(i, 1), (ys_s, ys_r), base + 3, at(y_down, zh))

    def y_last(i, q):
        base = 16 * i + 4 * q
        for part in range(2):
            arrived(wb.at[at((y + 2) & 3, zh_of[q]), rows(i, part)], ys_r.at[base + 2 + part])

    x_up, x_down, x_far = (x + 1) & 3, (x + 3) & 3, (x + 2) & 3

    def tat(xx, zz, cc):
        return xx * 4 + zz * 2 + cc

    zl_of = (zl, 1 - zl)

    def o_core(slot, idx):
        send(ogb.at[slot], ogb.at[slot], oc_s.at[idx], oc_r.at[idx], dp, tp ^ 1)

    def o_x(q):
        slot = tat(x, zl_of[q], core)
        send(ogb.at[slot], ogb.at[slot], ox_s.at[4 * q], ox_r.at[4 * q], dp, tat(x_up, zl, core))
        send(ogb.at[slot], ogb.at[slot], ox_s.at[4 * q + 1], ox_r.at[4 * q + 1], dp, tat(x_down, zl, core))

    def o_part(slot, part):
        return ogb.at[slot, pl.ds(part * (TOK // 2), TOK // 2)]

    def o_forward(q):
        slot = tat(x_down, zl_of[q], core)
        arrived(ogb.at[slot], ox_r.at[4 * q])
        ref = o_part(slot, 0)
        send(ref, ref, ox_s.at[4 * q + 2], ox_r.at[4 * q + 2], dp, tat(x_up, zl, core))
        o_core(slot, 2 + 3 * q)
        slot = tat(x_up, zl_of[q], core)
        arrived(ogb.at[slot], ox_r.at[4 * q + 1])
        ref = o_part(slot, 1)
        send(ref, ref, ox_s.at[4 * q + 3], ox_r.at[4 * q + 3], dp, tat(x_down, zl, core))
        o_core(slot, 3 + 3 * q)

    def o_last(q):
        slot = tat(x_far, zl_of[q], core)
        for part in range(2):
            arrived(o_part(slot, part), ox_r.at[4 * q + 2 + part])
        o_core(slot, 4 + 3 * q)

    def o_all():
        other = 1 - core
        arrived(ogb.at[tat(x, zl, other)], oc_r.at[0])
        arrived(ogb.at[tat(x, 1 - zl, other)], oc_r.at[1])
        for q in range(2):
            for k, xx in enumerate((x_down, x_up, x_far)):
                arrived(ogb.at[tat(xx, zl_of[q], other)], oc_r.at[2 + 3 * q + k])

    def exchange(idx, src_of, dst_of, axis):
        for k in range(1, N):
            d, t = (dp ^ k, tp) if axis == "dp" else (dp, tp ^ k)
            peer = d if axis == "dp" else t
            remote(src_of(peer), dst_of(k), small_s.at[idx], small_r.at[idx], d, t).start()

    def exchanged(idx, fifteen):
        copy = remote(fifteen, fifteen, small_s.at[idx], small_r.at[idx], dp, tp ^ 1)
        copy.wait_recv()
        copy.wait_send()

    z_own(0)
    send(ogb.at[tp], ogb.at[tp], oz_s, oz_r, dp, tat(x, 1 - zl, core))
    o_x(0)
    y_send(0, 0)
    o_core(tp, 0)
    z_own(1)
    y_send(1, 0)
    z_own(2)
    y_send(2, 0)

    def early():
        for n in range(2, 6):
            loads[n].wait()
        exchange(1, lambda peer: qb.at[peer], lambda k: qj.at[tp], "tp")
        sel0, sel1 = spread(0), spread(1)
        acc[...] = dot(inb[...], dot(inf_ref[...], sel0).astype(jnp.bfloat16))

        @pl.loop(0, NCH)
        def _(i):
            lanes = pl.ds(pl.multiple_of(i * CH, CH), CH)
            frows = pl.ds(pl.multiple_of(i * CH, CH), CH)
            g = gb[:, lanes].astype(jnp.float32)
            u = ub[:, lanes].astype(jnp.float32)
            s = jax.nn.sigmoid(g)
            activated = g * s
            ab[i, :, :CH] = u * s * (1.0 + g * (1.0 - s))
            ab[i, :, CH:] = activated
            hi, lo = split(activated * u)
            hfp = dot(hf_ref[frows, :], sel1).astype(jnp.bfloat16)
            acc[...] += dot(hi, hfp) + dot(lo, hfp)
            for h, sel in enumerate((sel0, sel1)):
                fp[h, i, :CH, :] = dot(gf_ref[frows, :], sel).astype(jnp.bfloat16)
                fp[h, i, CH:, :] = dot(uf_ref[frows, :], sel).astype(jnp.bfloat16)

        pih_msg[...] = acc[...].T.reshape(N, 8, TOK)
        exchange(0, lambda peer: pih_msg.at[peer], lambda k: pih_rcv.at[k - 1], "tp")

    def middle():
        exchanged(0, pih_rcv)
        total = pih_msg[tp]
        for k in range(N - 1):
            total = total + pih_rcv[k]
        iph[tp] = total
        exchange(2, lambda peer: iph.at[tp], lambda k: iph.at[tp], "tp")

    def mask():
        row, _ = iota2((4, TOK))
        return jnp.where(ids_ref[...] == dp * 4 + row, 1.0, 0.0)

    def by_example(dst, cols):
        m = mask()
        for jl in range(2):
            for jh in range(2):
                r = 8 * jl + 4 * jh
                jj = 2 * jh + jl
                dst[r : r + 4, :] = m * cols[jj : jj + 1, :]

    def iph2():
        return iph[...].reshape(N * 8, TOK)

    def output_side():
        loads[6].wait()
        sel0 = spread(0)
        acc[...] = jnp.zeros_like(acc)

        @pl.loop(0, N)
        def _(k):
            ofp = dot(ofb[pl.ds(pl.multiple_of(k * DS, DS), DS), :], sel0).astype(jnp.bfloat16)
            acc[...] += dot(ogb[k], ofp)

        opt[...] = acc[...].T.reshape(N, 8, TOK)
        by_example(omat, opt[tp])
        exchanged(2, iph.at[pl.ds(0, N - 1)])
        t2[...] = dot_nt(omat[...], iph2(), HIGHEST)
        exchanged(1, qj.at[pl.ds(0, N - 1)])
        qj[tp] = qb[tp]
        gacc[...] = jnp.zeros_like(gacc)

    def compute(i):
        for q in range(4):
            y_last(i, q)
        acc[...] = jnp.zeros_like(acc)

        @pl.loop(0, N)
        def _(k):
            acc[...] += dot_nt(ogb[k], wb[k, rows(i), :])

        for h in range(2):
            tok = slice(h * (TOK // 2), (h + 1) * (TOK // 2))
            c = acc[tok, :]
            hi_g, lo_g = split(c * ab[i, tok, :CH])
            hi_u, lo_u = split(c * ab[i, tok, CH:])
            gacc[...] += (
                dot(hi_g, fp[h, i, :CH, :]) + dot(lo_g, fp[h, i, :CH, :])
                + dot(hi_u, fp[h, i, CH:, :]) + dot(lo_u, fp[h, i, CH:, :])
            )

    early()
    for i in range(NCH + 3):
        if i < NCH:
            z_forward(i)
            y_send(i, 1)
            y_send(i, 2)
            if i + 3 < NCH:
                z_own(i + 3)
                y_send(i + 3, 0)
        if i == 0:
            slot = tat(x, 1 - zl, core)
            arrived(ogb.at[slot], oz_r)
            o_x(1)
            o_core(slot, 1)
        if i == 1:
            o_forward(0)
            middle()
        if i == 2:
            o_forward(1)
            o_last(0)
        if i == 3:
            o_last(1)
        if 1 <= i <= NCH:
            z_last(i - 1)
            y_send(i - 1, 3)
            for q in range(3):
                y_forward(i - 1, q)
        if 2 <= i <= NCH + 1:
            y_forward(i - 2, 3)
        if i == 3:
            o_all()
            output_side()
        if i >= 3:
            compute(i - 3)

    gmsg[...] = gacc[...].T.reshape(N, 8, TOK // 2)
    exchange(3, lambda peer: gmsg.at[peer], lambda k: grcv.at[k - 1], "tp")
    for copy in pending:
        copy.wait_send()
    exchanged(3, grcv)
    total = gmsg[tp]
    for k in range(N - 1):
        total = total + grcv[k]
    by_example(gmat, jnp.concatenate([total[0:4, :], total[4:8, :]], axis=1))
    t1 = dot_nt(gmat[...], iph2(), HIGHEST)
    _, lane = iota2((16, 128))
    both = jnp.where(((lane >> 2) & 1) == 0, t1, t2[...])
    row, col = iota2((128, 128))
    feature = ((row >> 3) << 2) + (row & 3)
    piece = jnp.zeros((8, 128), jnp.float32)
    for jl in range(2):
        place = jnp.where(col == jl * 64 + feature, 1.0, 0.0)
        piece = piece + dot(both[8 * jl : 8 * jl + 8, :], place, HIGHEST)
    pall[dp] = piece
    exchange(4, lambda peer: pall.at[dp], lambda k: pall.at[dp], "dp")
    exchanged(4, pall.at[pl.ds(0, N - 1)])
    sketch = pall[...].reshape(128, 128)
    hi, lo = split(sketch)
    squares = dot_nt(jnp.ones((8, 128), jnp.float32), sketch * sketch, HIGHEST)
    r = []
    for jh in range(2):
        qq = qj[:, :, 128 * jh : 128 * jh + 128].reshape(N * 32, 128)
        r.append(dot_nt(qq, hi) + dot_nt(qq, lo))
    _, lane = iota2((N * 32, 128))
    part = jnp.where(((lane >> 2) & 1) == 0, r[0], r[1])
    scm[:, 0:32, :] = part.reshape(N, 32, 128)
    scm[:, 32:40, :] = jnp.broadcast_to(squares[None], (N, 8, 128))
    exchange(5, lambda peer: scm.at[peer], lambda k: scr.at[k - 1], "tp")
    exchanged(5, scr)
    total = scm[tp]
    for k in range(N - 1):
        total = total + scr[k]
    row, col = iota2((64, 128))
    pick = jnp.where(((row >> 2) == (col >> 3)) & ((row & 3) == (col & 3)), 1.0, 0.0)
    full = dot_nt(pick, total, HIGHEST)
    scale = lax.rsqrt(full[:, 32:33] * (1.0 / 4096.0) + 1e-06) * (1.0 / 64.0)
    out_ref[...] = full[:, 0:32] * scale


def local(
    inputs, gate_pre, up_pre, out_grads, down_weight, example_ids,
    input_factor, gate_factor, up_factor, hidden_factor, output_factor, queries,
):
    by_column = queries.reshape(32, 64, N, 4).transpose(2, 0, 3, 1).reshape(N, 32, 256)
    hbm = pl.BlockSpec(memory_space=pl.ANY)
    vmem = pl.BlockSpec(memory_space=pltpu.VMEM)
    bf16, f32 = jnp.bfloat16, jnp.float32
    dma = pltpu.SemaphoreType.DMA
    return pl.pallas_call(
        kernel,
        out_shape=jax.ShapeDtypeStruct((64, 32), f32),
        in_specs=[hbm, hbm, hbm, hbm, hbm, vmem, vmem, vmem, vmem, vmem, hbm, hbm],
        out_specs=vmem,
        scratch_shapes=[
            pltpu.VMEM((N, TOK, DS), bf16),
            pltpu.VMEM((N, FS, DS), bf16),
            pltpu.VMEM((TOK, DS), bf16),
            pltpu.VMEM((TOK, FS), bf16),
            pltpu.VMEM((TOK, FS), bf16),
            pltpu.VMEM((N * DS, 64), bf16),
            pltpu.VMEM((N, 32, 256), bf16),
            pltpu.VMEM((NCH, TOK, 2 * CH), f32),
            pltpu.VMEM((2, NCH, 2 * CH, 128), bf16),
            pltpu.VMEM((TOK, 128), f32),
            pltpu.VMEM((N, 8, TOK), f32),
            pltpu.VMEM((N - 1, 8, TOK), f32),
            pltpu.VMEM((N, 8, TOK), f32),
            pltpu.VMEM((N, 8, TOK), f32),
            pltpu.VMEM((16, TOK), f32),
            pltpu.VMEM((16, TOK), f32),
            pltpu.VMEM((16, 128), f32),
            pltpu.VMEM((TOK // 2, 128), f32),
            pltpu.VMEM((N, 8, TOK // 2), f32),
            pltpu.VMEM((N - 1, 8, TOK // 2), f32),
            pltpu.VMEM((N, 8, 128), f32),
            pltpu.VMEM((N, 32, 256), bf16),
            pltpu.VMEM((N, 40, 128), f32),
            pltpu.VMEM((N - 1, 40, 128), f32),
            dma((7,)),
            dma((4 * NCH,)),
            dma((4 * NCH,)),
            dma((16 * NCH,)),
            dma((16 * NCH,)),
            dma,
            dma,
            dma((8,)),
            dma((8,)),
            dma((8,)),
            dma((8,)),
            dma((6,)),
            dma((6,)),
        ],
        compiler_params=pltpu.CompilerParams(
            collective_id=0, has_side_effects=True, vmem_limit_bytes=60 * 1024 * 1024
        ),
        cost_estimate=pl.CostEstimate(
            flops=2 * TOK * FS * N * DS, bytes_accessed=8 * 1024 * 1024, transcendentals=TOK * FS
        ),
        name="gather_and_score",
    )(
        inputs, gate_pre, up_pre, out_grads, down_weight, example_ids.reshape(1, TOK),
        input_factor, gate_factor, up_factor, hidden_factor, output_factor, by_column,
    )


def solution(mesh):
    return jax.shard_map(
        local,
        mesh=mesh,
        in_specs=(
            P("dp", "tp"),
            P("dp", "tp"),
            P("dp", "tp"),
            P("dp", "tp"),
            P("tp", "dp"),
            P("dp"),
            P("tp", None),
            P("tp", None),
            P("tp", None),
            P("tp", None),
            P(),
            P(("dp", "tp"), None),
        ),
        out_specs=P(None, ("dp", "tp")),
        check_vma=False,
    )
```

time: 481 us -> 208 us (0.43); the launches traced: 474 us -> 207 us
  waiting for transfers between devices: 377 us -> 0 us
  Pallas kernels: 0 us -> 193 us
  matrix products: 42.7 us -> 0 us
  blocking collectives: 40.3 us -> 0 us
  local copies, waits for them, and re-layouts: 0.26 us -> 14.1 us
  between operations: 13.2 us -> 0.04 us
    all_gather x2 -> x0, waiting for transfers between devices: 264 us -> none  [the longest x1 191 us: local(): lax.all_gather(down_weight, 'dp', axis=1, tiled=True)]
    pallas_call x0 -> x1, Pallas kernels: none -> 193 us  [local(): pl.pallas_call(kernel, out_shape=jax.ShapeDtypeStruct((64, 32), f32), in_...]
    psum x1 -> x0, waiting for transfers between devices: 112 us -> none  [local(): lax.psum((input_local, grad_local, hidden_local), 'tp')]
    dot_general x9 -> x0, matrix products: 42.7 us -> none  [the longest x1 17.8 us: local(): lax.dot_general(full_grads, lax.all_gather(down_weight, 'dp', axis=1, til...]
    all_gather x1 -> x0, blocking collectives: 40.3 us -> none  [local(): every_unit = lax.all_gather(unit_sketch, 'dp', axis=0, tiled=True)]
    unnamed x15 -> x10, local copies, waits for them, and re-layouts: 0.15 us -> 9.06 us
  transfers between devices with their start and end apart: 3 -> 0, of which waited for: 3 -> 0; matrix products, arithmetic and copies ran while one was open for 3% -> 0% of each run, Pallas kernels for 0% -> 0%
where the time goes in v1:
time: 208 us; the launch traced here: 207 us
  Pallas kernels  193 us (93%)
  local copies, waits for them, and re-layouts  14.1 us (7%)
    pallas_call x1, Pallas kernels, local(): pl.pallas_call(kernel, out_shape=jax.ShapeDtypeStruct((64, 32), f32), in_...  193 us
    unnamed x10, local copies, waits for them, and re-layouts  9.06 us

profile of v1, /device:TPU:1, one launch (start us, length us, event | category | flops | bytes accessed | tf_op | source)
XLA Modules:
  0.0 207.5 jit_solution(10027899036066346697)
XLA Ops:
  0.0 0.0 copy-start.1
  0.0 1.3 reshape.9.ids_ref
  1.3 1.6 copy.22.inf_ref
  2.9 1.7 copy.23.gf_ref
  4.6 1.7 copy.24.uf_ref
  6.4 1.7 copy.25.hf_ref
  8.1 0.0 copy-done.1
  8.1 0.5 copy.20
  8.6 0.0 copy-start
  8.6 1.2 copy.21
  9.8 1.1 reshape.11.q_hbm
  10.9 0.0 copy-done
  10.9 1.8 copy.26.of_hbm
  12.7 193.3 %gather_and_score.1 = f32[64,32]{1,0:T(8,128)} custom-call(bf16[768,512]{1,0:T(8,128)(2,1)} %in_hbm.1, bf16[768,896]{1,0:T(8,128)(2,1)} %gate_hbm.1, bf16[768,896]{1,0:T(8,128)(2,1)} %up_hbm.1, bf16[768,512]{1,0:T(8,128)(2,1)} %og_hbm.1, bf16[896,512]{1,0:T(8,128)(2,1)} %w_hbm.1, s32[1,768]{1,0:T(1,128)} %reshape.9.ids_ref, bf16[512,64]{1,0:T(8,128)(2,1)} %copy.22.inf_ref, ...), custom_call_target="tpu_custom_call" | custom-call | flops 11274289152 | bytes 8388608 | tf_op jit(solution)/shard_map/gather_and_score/pallas_call | solution.py:383
  206.0 1.4 copy.27
Async XLA Ops:
  0.0 8.1 %copy-start.1 = (bf16[32,4096]{1,0:T(8,128)(2,1)S(1)}, bf16[32,4096]{1,0:T(8,128)(2,1)}, u32[]{:S(2)}) copy-start(bf16[32,4096]{1,0:T(8,128)(2,1)} %param.23) | copy-start | bytes 786436
  8.6 2.3 %copy-start = (bf16[8192,64]{0,1:T(8,128)(2,1)S(1)}, bf16[8192,64]{0,1:T(8,128)(2,1)}, u32[]{:S(2)}) copy-start(bf16[8192,64]{0,1:T(8,128)(2,1)} %param.22) | copy-start | bytes 3145732

commit v2 on v1

--- a/solution.py
+++ b/solution.py
@@ -12,7 +12,10 @@
 FS = 896
 CH = 128
 NCH = FS // CH
-HALF = CH // 2
+YF = NCH - 1
+YR = 96
+START = (0, 128, 256, 384, 512, 768, 768 - YR)
+LENGTH = (128, 128, 128, 128, 256 - YR, 128, YR)
 N = 16
 MESH = pl.DeviceIdType.MESH
 HIGHEST = lax.Precision.HIGHEST
@@ -41,15 +44,15 @@
 
 
 def spread(kind):
-    row, col = iota2((64, 128))
-    hit = (row == ((col >> 3) << 2) + (col & 3)) & (((col >> 2) & 1) == kind)
+    row, col = iota2((128, 64))
+    hit = (col == ((row >> 3) << 2) + (row & 3)) & (((row >> 2) & 1) == kind)
     return jnp.where(hit, 1.0, 0.0).astype(jnp.bfloat16)
 
 
 def kernel(
     in_hbm, gate_hbm, up_hbm, og_hbm, w_hbm, ids_ref, inf_ref, gf_ref, uf_ref, hf_ref, of_hbm, q_hbm,
     out_ref,
-    ogb, wb, inb, gb, ub, ofb, qb, ab, fp, acc, pih_msg, pih_rcv, iph, opt, gmat, omat, t2,
+    ogb, wb, inb, gb, ub, ofb, qn, qt, qb, ab, fp, acc, acc2, pih_msg, pih_rcv, iph, opt, gmat, omat, t2,
     gacc, gmsg, grcv, pall, qj, scm, scr,
     loc_sem, zs_s, zs_r, ys_s, ys_r, oz_s, oz_r, ox_s, ox_r, oc_s, oc_r, small_s, small_r,
 ):
@@ -79,7 +82,7 @@
     loads = []
     for n, (src, dst) in enumerate((
         (w_hbm, wb.at[dp]), (og_hbm, ogb.at[tp]), (in_hbm, inb), (gate_hbm, gb), (up_hbm, ub),
-        (q_hbm, qb), (of_hbm, ofb),
+        (q_hbm, qn), (of_hbm, ofb),
     )):
         copy = pltpu.make_async_copy(src, dst, loc_sem.at[n])
         copy.start()
@@ -101,8 +104,8 @@
 
     def rows(i, part=None):
         if part is None:
-            return pl.ds(i * CH, CH)
-        return pl.ds(i * CH + part * HALF, HALF)
+            return pl.ds(START[i], LENGTH[i])
+        return pl.ds(START[i] + part * (LENGTH[i] // 2), LENGTH[i] // 2)
 
     def w_send(block, r, sems, idx, target):
         ss, rs = sems
@@ -139,6 +142,39 @@
         base = 16 * i + 4 * q
         for part in range(2):
             arrived(wb.at[at((y + 2) & 3, zh_of[q]), rows(i, part)], ys_r.at[base + 2 + part])
+
+    y_of = (y, y_down, y_up, (y + 2) & 3)
+
+    def yo_send():
+        w_send(dp, rows(YF), (zs_s, zs_r), 4 * YF, at(y_up, zh))
+        w_send(dp, rows(YF), (zs_s, zs_r), 4 * YF + 1, at(y_down, zh))
+
+    def yo_forward():
+        arrived(wb.at[at(y_down, zh), rows(YF)], zs_r.at[4 * YF])
+        w_send(at(y_down, zh), rows(YF, 0), (zs_s, zs_r), 4 * YF + 2, at(y_up, zh))
+        arrived(wb.at[at(y_up, zh), rows(YF)], zs_r.at[4 * YF + 1])
+        w_send(at(y_up, zh), rows(YF, 1), (zs_s, zs_r), 4 * YF + 3, at(y_down, zh))
+
+    def yo_last():
+        for part in range(2):
+            arrived(wb.at[at(y_of[3], zh), rows(YF, part)], zs_r.at[4 * YF + 2 + part])
+
+    def zq_send(q):
+        base = 16 * YF + 4 * q
+        w_send(at(y_of[q], zh), rows(YF), (ys_s, ys_r), base, at(y, zh_up))
+        w_send(at(y_of[q], zh), rows(YF), (ys_s, ys_r), base + 1, at(y, zh_down))
+
+    def zq_forward(q):
+        base = 16 * YF + 4 * q
+        arrived(wb.at[at(y_of[q], zh_down), rows(YF)], ys_r.at[base])
+        w_send(at(y_of[q], zh_down), rows(YF, 0), (ys_s, ys_r), base + 2, at(y, zh_up))
+        arrived(wb.at[at(y_of[q], zh_up), rows(YF)], ys_r.at[base + 1])
+        w_send(at(y_of[q], zh_up), rows(YF, 1), (ys_s, ys_r), base + 3, at(y, zh_down))
+
+    def zq_last(q):
+        base = 16 * YF + 4 * q
+        for part in range(2):
+            arrived(wb.at[at(y_of[q], zh_of[3]), rows(YF, part)], ys_r.at[base + 2 + part])
 
     x_up, x_down, x_far = (x + 1) & 3, (x + 3) & 3, (x + 2) & 3
 
@@ -199,23 +235,21 @@
     send(ogb.at[tp], ogb.at[tp], oz_s, oz_r, dp, tat(x, 1 - zl, core))
     o_x(0)
     y_send(0, 0)
+    yo_send()
     o_core(tp, 0)
     z_own(1)
-    y_send(1, 0)
-    z_own(2)
-    y_send(2, 0)
+    for i in range(1, YF):
+        y_send(i, 0)
 
     def early():
-        for n in range(2, 6):
+        for n in range(2, 5):
             loads[n].wait()
-        exchange(1, lambda peer: qb.at[peer], lambda k: qj.at[tp], "tp")
         sel0, sel1 = spread(0), spread(1)
-        acc[...] = dot(inb[...], dot(inf_ref[...], sel0).astype(jnp.bfloat16))
+        acc[...] = dot_nt(inb[...], dot(sel0, inf_ref[...]).astype(jnp.bfloat16))
 
         @pl.loop(0, NCH)
         def _(i):
             lanes = pl.ds(pl.multiple_of(i * CH, CH), CH)
-            frows = pl.ds(pl.multiple_of(i * CH, CH), CH)
             g = gb[:, lanes].astype(jnp.float32)
             u = ub[:, lanes].astype(jnp.float32)
             s = jax.nn.sigmoid(g)
@@ -223,14 +257,31 @@
             ab[i, :, :CH] = u * s * (1.0 + g * (1.0 - s))
             ab[i, :, CH:] = activated
             hi, lo = split(activated * u)
-            hfp = dot(hf_ref[frows, :], sel1).astype(jnp.bfloat16)
-            acc[...] += dot(hi, hfp) + dot(lo, hfp)
+            hfp = dot(sel1, hf_ref[:, lanes]).astype(jnp.bfloat16)
+            acc[...] += dot_nt(hi, hfp) + dot_nt(lo, hfp)
             for h, sel in enumerate((sel0, sel1)):
-                fp[h, i, :CH, :] = dot(gf_ref[frows, :], sel).astype(jnp.bfloat16)
-                fp[h, i, CH:, :] = dot(uf_ref[frows, :], sel).astype(jnp.bfloat16)
+                fp[h, i, :, :CH] = dot(sel, gf_ref[:, lanes]).astype(jnp.bfloat16)
+                fp[h, i, :, CH:] = dot(sel, uf_ref[:, lanes]).astype(jnp.bfloat16)
 
         pih_msg[...] = acc[...].T.reshape(N, 8, TOK)
         exchange(0, lambda peer: pih_msg.at[peer], lambda k: pih_rcv.at[k - 1], "tp")
+
+    def spread_queries():
+        loads[5].wait()
+        row, col = iota2((128, 128))
+        hit = col == ((row & 1) << 6) + ((row >> 3) << 2) + ((row >> 1) & 3)
+        place = jnp.where(hit, 1.0, 0.0).astype(jnp.bfloat16)
+        for m in range(32):
+            moved = dot_nt(place, qn[:, 128 * m : 128 * m + 128])
+            qt[:, 8 * m : 8 * m + 8, 0:32] = moved.reshape(N, 8, 32)
+
+        @pl.loop(0, N)
+        def _(k):
+            for half in range(2):
+                turned = qt[k, 128 * half : 128 * half + 128, :].T
+                qb[k, :, 128 * half : 128 * half + 128] = turned[0:32, :].astype(jnp.bfloat16)
+
+        exchange(1, lambda peer: qb.at[peer], lambda k: qj.at[tp], "tp")
 
     def middle():
         exchanged(0, pih_rcv)
@@ -242,15 +293,12 @@
 
     def mask():
         row, _ = iota2((4, TOK))
-        return jnp.where(ids_ref[...] == dp * 4 + row, 1.0, 0.0)
+        return jnp.where(ids_ref[...].reshape(1, TOK) == dp * 4 + row, 1.0, 0.0)
 
     def by_example(dst, cols):
         m = mask()
-        for jl in range(2):
-            for jh in range(2):
-                r = 8 * jl + 4 * jh
-                jj = 2 * jh + jl
-                dst[r : r + 4, :] = m * cols[jj : jj + 1, :]
+        for jj in range(4):
+            dst[4 * jj : 4 * jj + 4, :] = m * cols[jj : jj + 1, :]
 
     def iph2():
         return iph[...].reshape(N * 8, TOK)
@@ -262,8 +310,8 @@
 
         @pl.loop(0, N)
         def _(k):
-            ofp = dot(ofb[pl.ds(pl.multiple_of(k * DS, DS), DS), :], sel0).astype(jnp.bfloat16)
-            acc[...] += dot(ogb[k], ofp)
+            ofp = dot(sel0, ofb[:, pl.ds(pl.multiple_of(k * DS, DS), DS)]).astype(jnp.bfloat16)
+            acc[...] += dot_nt(ogb[k], ofp)
 
         opt[...] = acc[...].T.reshape(N, 8, TOK)
         by_example(omat, opt[tp])
@@ -273,59 +321,99 @@
         qj[tp] = qb[tp]
         gacc[...] = jnp.zeros_like(gacc)
 
-    def compute(i):
-        for q in range(4):
-            y_last(i, q)
-        acc[...] = jnp.zeros_like(acc)
-
-        @pl.loop(0, N)
-        def _(k):
-            acc[...] += dot_nt(ogb[k], wb[k, rows(i), :])
-
+    def multiply(place, width, ks, first):
+        out = acc2.at[:, pl.ds(0, width * CH)]
+        if first:
+            out[...] = jnp.zeros_like(out)
+
+        @pl.loop(0, 4)
+        def _(n):
+            for k in ks:
+                slot = k(n)
+                out[...] += dot_nt(ogb[slot], wb[slot, pl.ds(place * CH, width * CH), :])
+
+    def project(place, half):
         for h in range(2):
             tok = slice(h * (TOK // 2), (h + 1) * (TOK // 2))
-            c = acc[tok, :]
-            hi_g, lo_g = split(c * ab[i, tok, :CH])
-            hi_u, lo_u = split(c * ab[i, tok, CH:])
+            c = acc2[tok, half * CH : half * CH + CH]
+            hi_g, lo_g = split(c * ab[place, tok, :CH])
+            hi_u, lo_u = split(c * ab[place, tok, CH:])
             gacc[...] += (
-                dot(hi_g, fp[h, i, :CH, :]) + dot(lo_g, fp[h, i, :CH, :])
-                + dot(hi_u, fp[h, i, CH:, :]) + dot(lo_u, fp[h, i, CH:, :])
+                dot_nt(hi_g, fp[h, place, :, :CH]) + dot_nt(lo_g, fp[h, place, :, :CH])
+                + dot_nt(hi_u, fp[h, place, :, CH:]) + dot_nt(lo_u, fp[h, place, :, CH:])
             )
 
+    def slot_of(q):
+        return lambda n: n * 4 + zh_of[q]
+
+    every = [slot_of(q) for q in range(4)]
+
+    def compute_pair(place):
+        multiply(place, 2, every, True)
+        project(place, 0)
+        project(place + 1, 1)
+
+    def y_wait(i, qs):
+        for q in qs:
+            y_last(i, q)
+
     early()
-    for i in range(NCH + 3):
-        if i < NCH:
+    for i in range(YF + 2):
+        if i < YF:
             z_forward(i)
             y_send(i, 1)
             y_send(i, 2)
-            if i + 3 < NCH:
-                z_own(i + 3)
-                y_send(i + 3, 0)
+            if i + 2 < YF:
+                z_own(i + 2)
+        if 1 <= i <= YF:
+            z_last(i - 1)
+            y_send(i - 1, 3)
         if i == 0:
+            yo_forward()
+            for k in range(YF):
+                y_forward(k, 0)
+            o_forward(0)
+        if 1 <= i <= YF:
+            y_forward(i - 1, 1)
+            y_forward(i - 1, 2)
+        if 2 <= i <= YF + 1:
+            y_forward(i - 2, 3)
+        if i == 1:
             slot = tat(x, 1 - zl, core)
             arrived(ogb.at[slot], oz_r)
             o_x(1)
             o_core(slot, 1)
-        if i == 1:
-            o_forward(0)
             middle()
-        if i == 2:
+            spread_queries()
+        if i == 3:
             o_forward(1)
             o_last(0)
-        if i == 3:
+        if i == 4:
+            yo_last()
+            for q in range(4):
+                zq_send(q)
             o_last(1)
-        if 1 <= i <= NCH:
-            z_last(i - 1)
-            y_send(i - 1, 3)
-            for q in range(3):
-                y_forward(i - 1, q)
-        if 2 <= i <= NCH + 1:
-            y_forward(i - 2, 3)
-        if i == 3:
             o_all()
             output_side()
-        if i >= 3:
-            compute(i - 3)
+        if i == 5:
+            for q in range(4):
+                zq_forward(q)
+            y_wait(0, range(4))
+            y_wait(1, range(4))
+            compute_pair(0)
+        if i == 6:
+            y_wait(2, range(4))
+            y_wait(3, range(4))
+            compute_pair(2)
+            y_wait(4, range(4))
+            for q in range(4):
+                zq_last(q)
+            compute_pair(4)
+    y_wait(5, range(3))
+    multiply(6, 1, every[:3], True)
+    y_wait(5, [3])
+    multiply(6, 1, every[3:], False)
+    project(6, 0)
 
     gmsg[...] = gacc[...].T.reshape(N, 8, TOK // 2)
     exchange(3, lambda peer: gmsg.at[peer], lambda k: grcv.at[k - 1], "tp")
@@ -341,11 +429,15 @@
     both = jnp.where(((lane >> 2) & 1) == 0, t1, t2[...])
     row, col = iota2((128, 128))
     feature = ((row >> 3) << 2) + (row & 3)
-    piece = jnp.zeros((8, 128), jnp.float32)
-    for jl in range(2):
-        place = jnp.where(col == jl * 64 + feature, 1.0, 0.0)
-        piece = piece + dot(both[8 * jl : 8 * jl + 8, :], place, HIGHEST)
-    pall[dp] = piece
+    wanted = ((col >> 3) << 1) + (col & 1)
+    erow, lane = iota2((16, 128))
+    for half in range(2):
+        place = jnp.where(feature == wanted + 32 * half, 1.0, 0.0)
+        moved = dot(both, place, HIGHEST)
+        moved = jnp.where((erow >> 2) == ((lane >> 1) & 3), moved, 0.0)
+        pall[dp, 4 * half : 4 * half + 4, :] = (
+            moved[0:4, :] + moved[4:8, :] + moved[8:12, :] + moved[12:16, :]
+        )
     exchange(4, lambda peer: pall.at[dp], lambda k: pall.at[dp], "dp")
     exchanged(4, pall.at[pl.ds(0, N - 1)])
     sketch = pall[...].reshape(128, 128)
@@ -366,23 +458,22 @@
         total = total + scr[k]
     row, col = iota2((64, 128))
     pick = jnp.where(((row >> 2) == (col >> 3)) & ((row & 3) == (col & 3)), 1.0, 0.0)
-    full = dot_nt(pick, total, HIGHEST)
-    scale = lax.rsqrt(full[:, 32:33] * (1.0 / 4096.0) + 1e-06) * (1.0 / 64.0)
-    out_ref[...] = full[:, 0:32] * scale
+    full = dot_nt(total, pick, HIGHEST)
+    scale = lax.rsqrt(full[32:33, :] * (1.0 / 4096.0) + 1e-06) * (1.0 / 64.0)
+    out_ref[...] = full[0:32, :] * scale
 
 
 def local(
     inputs, gate_pre, up_pre, out_grads, down_weight, example_ids,
     input_factor, gate_factor, up_factor, hidden_factor, output_factor, queries,
 ):
-    by_column = queries.reshape(32, 64, N, 4).transpose(2, 0, 3, 1).reshape(N, 32, 256)
     hbm = pl.BlockSpec(memory_space=pl.ANY)
     vmem = pl.BlockSpec(memory_space=pltpu.VMEM)
     bf16, f32 = jnp.bfloat16, jnp.float32
     dma = pltpu.SemaphoreType.DMA
     return pl.pallas_call(
         kernel,
-        out_shape=jax.ShapeDtypeStruct((64, 32), f32),
+        out_shape=jax.ShapeDtypeStruct((32, 64), f32),
         in_specs=[hbm, hbm, hbm, hbm, hbm, vmem, vmem, vmem, vmem, vmem, hbm, hbm],
         out_specs=vmem,
         scratch_shapes=[
@@ -391,11 +482,14 @@
             pltpu.VMEM((TOK, DS), bf16),
             pltpu.VMEM((TOK, FS), bf16),
             pltpu.VMEM((TOK, FS), bf16),
-            pltpu.VMEM((N * DS, 64), bf16),
+            pltpu.VMEM((64, N * DS), bf16),
+            pltpu.VMEM((32, 4096), bf16),
+            pltpu.VMEM((N, 256, 128), f32),
             pltpu.VMEM((N, 32, 256), bf16),
             pltpu.VMEM((NCH, TOK, 2 * CH), f32),
-            pltpu.VMEM((2, NCH, 2 * CH, 128), bf16),
+            pltpu.VMEM((2, NCH, 128, 2 * CH), bf16),
             pltpu.VMEM((TOK, 128), f32),
+            pltpu.VMEM((TOK, 2 * CH), f32),
             pltpu.VMEM((N, 8, TOK), f32),
             pltpu.VMEM((N - 1, 8, TOK), f32),
             pltpu.VMEM((N, 8, TOK), f32),
@@ -432,9 +526,9 @@
         ),
         name="gather_and_score",
     )(
-        inputs, gate_pre, up_pre, out_grads, down_weight, example_ids.reshape(1, TOK),
-        input_factor, gate_factor, up_factor, hidden_factor, output_factor, by_column,
-    )
+        inputs, gate_pre, up_pre, out_grads, down_weight, example_ids,
+        input_factor.T, gate_factor.T, up_factor.T, hidden_factor.T, output_factor.T, queries,
+    ).T
 
 
 def solution(mesh):

time: 208 us -> 161 us (0.77)
  Pallas kernels: 193 us -> 159 us
  local copies, waits for them, and re-layouts: 14.1 us -> 1.32 us
    pallas_call x1, Pallas kernels: 193 us -> 159 us  [local(): pl.pallas_call(kernel, out_shape=jax.ShapeDtypeStruct((32, 64), f32), in_...]
    unnamed x10 -> x1, local copies, waits for them, and re-layouts: 9.06 us -> 1.32 us
    reshape x2 -> x0, local copies, waits for them, and re-layouts: 2.39 us -> none  [the longest x1 1.31 us: local(): example_ids.reshape(1, TOK)]
where the time goes in v2:
time: 161 us
  Pallas kernels  159 us (99%)
    pallas_call x1, Pallas kernels, local(): pl.pallas_call(kernel, out_shape=jax.ShapeDtypeStruct((32, 64), f32), in_...  159 us

profile of v2, /device:TPU:1, one launch (start us, length us, event | category | flops | bytes accessed | tf_op | source)
XLA Modules:
  0.0 160.8 jit_solution(8554735323473803187)
XLA Ops:
  0.0 159.5 %gather_and_score.1 = f32[32,64]{1,0:T(8,128)} custom-call(bf16[768,512]{1,0:T(8,128)(2,1)} %in_hbm.1, bf16[768,896]{1,0:T(8,128)(2,1)} %gate_hbm.1, bf16[768,896]{1,0:T(8,128)(2,1)} %up_hbm.1, bf16[768,512]{1,0:T(8,128)(2,1)} %og_hbm.1, bf16[896,512]{1,0:T(8,128)(2,1)} %w_hbm.1, s32[768]{0:T(1024)} %ids_ref.1, bf16[64,512]{1,0:T(8,128)(2,1)} %bitcast.11, ...), custom_call_target="tpu_custom_call" | custom-call | flops 11274289152 | bytes 8388608 | tf_op jit(solution)/shard_map/gather_and_score/pallas_call | solution.py:474
  159.5 1.3 copy.14

commit v3 on v2

--- a/solution.py
+++ b/solution.py
@@ -110,7 +110,7 @@
     def w_send(block, r, sems, idx, target):
         ss, rs = sems
         ref = wb.at[block, r]
-        send(ref, ref, ss.at[idx], rs.at[idx], target, tp)
+        remote(ref, ref, ss, rs.at[idx], target, tp).start()
 
     def z_own(i):
         w_send(dp, rows(i), (zs_s, zs_r), 4 * i, at(y, zh_up))
@@ -221,7 +221,7 @@
                 arrived(ogb.at[tat(xx, zl_of[q], other)], oc_r.at[2 + 3 * q + k])
 
     def exchange(idx, src_of, dst_of, axis):
-        for k in range(1, N):
+        for k in (8, 9, 10, 11, 12, 13, 14, 15, 4, 5, 6, 7, 2, 3, 1):
             d, t = (dp ^ k, tp) if axis == "dp" else (dp, tp ^ k)
             peer = d if axis == "dp" else t
             remote(src_of(peer), dst_of(k), small_s.at[idx], small_r.at[idx], d, t).start()
@@ -321,8 +321,7 @@
         qj[tp] = qb[tp]
         gacc[...] = jnp.zeros_like(gacc)
 
-    def multiply(place, width, ks, first):
-        out = acc2.at[:, pl.ds(0, width * CH)]
+    def multiply(out, place, width, ks, first):
         if first:
             out[...] = jnp.zeros_like(out)
 
@@ -332,16 +331,12 @@
                 slot = k(n)
                 out[...] += dot_nt(ogb[slot], wb[slot, pl.ds(place * CH, width * CH), :])
 
-    def project(place, half):
+    def project(source, place, half):
         for h in range(2):
             tok = slice(h * (TOK // 2), (h + 1) * (TOK // 2))
-            c = acc2[tok, half * CH : half * CH + CH]
-            hi_g, lo_g = split(c * ab[place, tok, :CH])
-            hi_u, lo_u = split(c * ab[place, tok, CH:])
-            gacc[...] += (
-                dot_nt(hi_g, fp[h, place, :, :CH]) + dot_nt(lo_g, fp[h, place, :, :CH])
-                + dot_nt(hi_u, fp[h, place, :, CH:]) + dot_nt(lo_u, fp[h, place, :, CH:])
-            )
+            c = source[tok, half * CH : half * CH + CH]
+            hi, lo = split(jnp.concatenate([c * ab[place, tok, :CH], c * ab[place, tok, CH:]], axis=1))
+            gacc[...] += dot_nt(hi, fp[h, place]) + dot_nt(lo, fp[h, place])
 
     def slot_of(q):
         return lambda n: n * 4 + zh_of[q]
@@ -349,9 +344,9 @@
     every = [slot_of(q) for q in range(4)]
 
     def compute_pair(place):
-        multiply(place, 2, every, True)
-        project(place, 0)
-        project(place + 1, 1)
+        multiply(acc2, place, 2, every, True)
+        project(acc2, place, 0)
+        project(acc2, place + 1, 1)
 
     def y_wait(i, qs):
         for q in qs:
@@ -395,30 +390,41 @@
             o_last(1)
             o_all()
             output_side()
+            y_wait(0, range(4))
+            y_wait(1, range(4))
+            compute_pair(0)
         if i == 5:
             for q in range(4):
                 zq_forward(q)
-            y_wait(0, range(4))
-            y_wait(1, range(4))
-            compute_pair(0)
+            y_wait(2, range(4))
+            y_wait(3, range(3))
+            multiply(acc2, 2, 2, every[:3], True)
         if i == 6:
-            y_wait(2, range(4))
-            y_wait(3, range(4))
-            compute_pair(2)
-            y_wait(4, range(4))
-            for q in range(4):
-                zq_last(q)
-            compute_pair(4)
+            y_wait(3, [3])
+            multiply(acc2, 2, 2, every[3:], False)
+            project(acc2, 2, 0)
+            project(acc2, 3, 1)
+            y_wait(4, range(3))
+            multiply(acc2, 4, 2, every[:3], True)
     y_wait(5, range(3))
-    multiply(6, 1, every[:3], True)
+    multiply(acc, 6, 1, every[:3], True)
+    y_wait(4, [3])
+    for q in range(4):
+        zq_last(q)
+    multiply(acc2, 4, 2, every[3:], False)
+    project(acc2, 4, 0)
+    project(acc2, 5, 1)
     y_wait(5, [3])
-    multiply(6, 1, every[3:], False)
-    project(6, 0)
+    multiply(acc, 6, 1, every[3:], False)
+    project(acc, 6, 0)
 
     gmsg[...] = gacc[...].T.reshape(N, 8, TOK // 2)
     exchange(3, lambda peer: gmsg.at[peer], lambda k: grcv.at[k - 1], "tp")
     for copy in pending:
         copy.wait_send()
+    for sem, blocks in ((zs_s, 3), (ys_s, 12)):
+        ref = wb.at[pl.ds(0, blocks)]
+        remote(ref, ref, sem, sem, dp, tp ^ 1).wait_send()
     exchanged(3, grcv)
     total = gmsg[tp]
     for k in range(N - 1):
@@ -449,8 +455,11 @@
         r.append(dot_nt(qq, hi) + dot_nt(qq, lo))
     _, lane = iota2((N * 32, 128))
     part = jnp.where(((lane >> 2) & 1) == 0, r[0], r[1])
-    scm[:, 0:32, :] = part.reshape(N, 32, 128)
-    scm[:, 32:40, :] = jnp.broadcast_to(squares[None], (N, 8, 128))
+    down = (part + pltpu.roll(part, 124, 1)).reshape(N, 32, 128)
+    up = (part + pltpu.roll(part, 4, 1)).reshape(N, 32, 128)
+    _, lane = iota2((16, 128))
+    scm[:, 0:16, :] = jnp.where((((lane >> 2) & 1) == 0)[None], down[:, 0:16, :], up[:, 16:32, :])
+    scm[:, 16:24, :] = jnp.broadcast_to(squares[None], (N, 8, 128))
     exchange(5, lambda peer: scm.at[peer], lambda k: scr.at[k - 1], "tp")
     exchanged(5, scr)
     total = scm[tp]
@@ -458,9 +467,11 @@
         total = total + scr[k]
     row, col = iota2((64, 128))
     pick = jnp.where(((row >> 2) == (col >> 3)) & ((row & 3) == (col & 3)), 1.0, 0.0)
-    full = dot_nt(total, pick, HIGHEST)
-    scale = lax.rsqrt(full[32:33, :] * (1.0 / 4096.0) + 1e-06) * (1.0 / 64.0)
-    out_ref[...] = full[0:32, :] * scale
+    square = dot_nt(total[16:24, :], pick, HIGHEST)[0:1, :]
+    scale = lax.rsqrt(square * (1.0 / 4096.0) + 1e-06) * (1.0 / 64.0)
+    for half in range(2):
+        here = jnp.where(((col >> 2) & 1) == half, pick, 0.0)
+        out_ref[16 * half : 16 * half + 16, :] = dot_nt(total[0:16, :], here, HIGHEST) * scale
 
 
 def local(
@@ -502,12 +513,12 @@
             pltpu.VMEM((N - 1, 8, TOK // 2), f32),
             pltpu.VMEM((N, 8, 128), f32),
             pltpu.VMEM((N, 32, 256), bf16),
-            pltpu.VMEM((N, 40, 128), f32),
-            pltpu.VMEM((N - 1, 40, 128), f32),
+            pltpu.VMEM((N, 24, 128), f32),
+            pltpu.VMEM((N - 1, 24, 128), f32),
             dma((7,)),
+            dma,
             dma((4 * NCH,)),
-            dma((4 * NCH,)),
-            dma((16 * NCH,)),
+            dma,
             dma((16 * NCH,)),
             dma,
             dma,

time: 161 us -> 157 us (0.975)
  Pallas kernels: 159 us -> 156 us
    pallas_call x1, Pallas kernels: 159 us -> 156 us  [local(): pl.pallas_call(kernel, out_shape=jax.ShapeDtypeStruct((32, 64), f32), in_...]
where the time goes in v3:
time: 157 us
  Pallas kernels  156 us (99%)
    pallas_call x1, Pallas kernels, local(): pl.pallas_call(kernel, out_shape=jax.ShapeDtypeStruct((32, 64), f32), in_...  156 us

profile of v3, /device:TPU:1, one launch (start us, length us, event | category | flops | bytes accessed | tf_op | source)
XLA Modules:
  0.0 156.8 jit_solution(14756598071502361262)
XLA Ops:
  0.0 155.5 %gather_and_score.1 = f32[32,64]{1,0:T(8,128)} custom-call(bf16[768,512]{1,0:T(8,128)(2,1)} %in_hbm.1, bf16[768,896]{1,0:T(8,128)(2,1)} %gate_hbm.1, bf16[768,896]{1,0:T(8,128)(2,1)} %up_hbm.1, bf16[768,512]{1,0:T(8,128)(2,1)} %og_hbm.1, bf16[896,512]{1,0:T(8,128)(2,1)} %w_hbm.1, s32[768]{0:T(1024)} %ids_ref.1, bf16[64,512]{1,0:T(8,128)(2,1)} %bitcast.11, ...), custom_call_target="tpu_custom_call" | custom-call | flops 11274289152 | bytes 8388608 | tf_op jit(solution)/shard_map/gather_and_score/pallas_call | solution.py:485
  155.5 1.3 copy.14

commit v4 on v3

--- a/solution.py
+++ b/solution.py
@@ -390,12 +390,12 @@
             o_last(1)
             o_all()
             output_side()
+        if i == 5:
+            for q in range(4):
+                zq_forward(q)
             y_wait(0, range(4))
             y_wait(1, range(4))
             compute_pair(0)
-        if i == 5:
-            for q in range(4):
-                zq_forward(q)
             y_wait(2, range(4))
             y_wait(3, range(3))
             multiply(acc2, 2, 2, every[:3], True)

time: 157 us -> 155 us (0.987)
  Pallas kernels: 156 us -> 153 us
    pallas_call x1, Pallas kernels: 156 us -> 153 us  [local(): pl.pallas_call(kernel, out_shape=jax.ShapeDtypeStruct((32, 64), f32), in_...]
where the time goes in v4:
time: 155 us; the launch traced here: 154 us
  Pallas kernels  153 us (99%)
    pallas_call x1, Pallas kernels, local(): pl.pallas_call(kernel, out_shape=jax.ShapeDtypeStruct((32, 64), f32), in_...  153 us

profile of v4, /device:TPU:1, one launch (start us, length us, event | category | flops | bytes accessed | tf_op | source)
XLA Modules:
  0.0 154.5 jit_solution(14632793489790401844)
XLA Ops:
  0.0 153.1 %gather_and_score.1 = f32[32,64]{1,0:T(8,128)} custom-call(bf16[768,512]{1,0:T(8,128)(2,1)} %in_hbm.1, bf16[768,896]{1,0:T(8,128)(2,1)} %gate_hbm.1, bf16[768,896]{1,0:T(8,128)(2,1)} %up_hbm.1, bf16[768,512]{1,0:T(8,128)(2,1)} %og_hbm.1, bf16[896,512]{1,0:T(8,128)(2,1)} %w_hbm.1, s32[768]{0:T(1024)} %ids_ref.1, bf16[64,512]{1,0:T(8,128)(2,1)} %bitcast.11, ...), custom_call_target="tpu_custom_call" | custom-call | flops 11274289152 | bytes 8388608 | tf_op jit(solution)/shard_map/gather_and_score/pallas_call | solution.py:485
  153.1 1.3 copy.14
